TPU v7x, 512 devices: a whole 4x4x16 slice. The times are simulated.
512 devices in a mesh: mp: 16 (over z), trow: 4 (over x), tcol: 8 (over y, core).
Axes of the slice: x: 4, y: 4, z: 16, core: 2. Of those that a mesh axis runs over, the one named last changes fastest.
Arguments:
- gram: float32 [16, 4096, 4096], P('mp', 'trow', 'tcol'), as said below
- rhs: float32 [256, 4096], P(('mp', 'tcol'), 'trow'), may hold values from -6 to 6
- guess: float32 [256, 4096], P(('mp', 'tcol'), 'trow'), may hold values from -6 to 6
Outputs:
- merged: float32 [256, 4096], P(('mp', 'tcol'), 'trow')
- residual: float32 [256, 4096], P(('mp', 'tcol'), 'trow')
Inputs may be any that keep to these rules, and one draw needn't show every extreme that they name: gram holds 16 symmetric positive definite matrices, one per model.
All inputs are finite; a program needn't handle non-finite values.
Results may differ from a plain program's by a relative error of at most 0.0003.
Values sent between devices are 32-bit elements; how exact they have to be, the bound alone decides.
No kernel may reach another device: no remote copies, remote signals or barrier semaphores. Data moves between devices by JAX's collectives and lax.ppermute only.
A program may use at most 64 MiB of HBM per device.

v0:
```python
import jax
import jax.numpy as jnp
from jax import lax
from jax.sharding import Mesh, PartitionSpec as P

MP = ("zh", "zl")
PLANE = ("trow", "tcol")
HIGHEST = lax.Precision.HIGHEST


def dot(lhs, rhs, lhs_dim, rhs_dim):
    return lax.dot_general(
        lhs,
        rhs,
        (((lhs_dim,), (rhs_dim,)), ((), ())),
        precision=HIGHEST,
        preferred_element_type=jnp.float32,
    )


def exchange(pieces, axes):
    return lax.all_to_all(pieces, axes, 0, 0, tiled=True)


def spread(block, axes, count):
    return exchange(jnp.broadcast_to(block[None], (count,) + block.shape), axes)


def transposed(vector, sizes):
    trow, tcol = (sizes["trow"], sizes["tcol"])
    own, wide = vector.shape
    half = wide // 2
    core = lax.axis_index("tcol") % 2
    halves = (vector[:, :half], vector[:, half:])
    got = []
    for turn in range(2):
        pairs = []
        for i in range(trow):
            for j in range(tcol):
                q, h = (j // 2, j % 2)
                pairs.append((i * tcol + j, q * tcol + 2 * i + (h ^ turn)))
        low = core == turn
        sent = jnp.where(low, halves[0], halves[1])
        got.append(lax.ppermute(sent, PLANE, pairs))
    first = core == 0
    return jnp.stack([jnp.where(first, got[0], got[1]), jnp.where(first, got[1], got[0])])


def shards(sizes, gram, rhs, guess):
    zh, zl, trow, tcol = (sizes["zh"], sizes["zl"], sizes["trow"], sizes["tcol"])
    mp = zh * zl
    tile = gram[0]
    rows, cols = tile.shape
    own = rhs.shape[0]
    thin = cols // zh
    cut = (
        tile.reshape(zl, rows // zl, zh, thin)
        .transpose(2, 0, 1, 3)
        .reshape(mp * (rows // zl), thin)
    )
    part = lax.psum_scatter(cut, MP, scatter_dimension=0, tiled=True)
    total = lax.all_gather(part, "zl", axis=0, tiled=True)
    flipped = transposed(guess, sizes)
    over_mp = spread(flipped, MP, mp)
    over_mp = over_mp.transpose(1, 0, 2, 3).reshape(2 * mp * own, cols)
    block = spread(over_mp, "trow", trow).reshape(trow * 2 * mp * own, cols)
    terms = dot(block, tile, 1, 1)
    terms = exchange(terms.reshape(tcol, mp * own, rows), "tcol").sum(0)
    terms = exchange(terms.reshape(mp, own, rows), MP).sum(0)
    first = rhs - terms
    near = spread(first, "zh", zh).reshape(zh * own, rows)
    wide = spread(near, "tcol", tcol).reshape(tcol * zh * own, rows)
    second = spread(dot(wide, total, 1, 0), "trow", trow).sum(0)
    terms = dot(second, total, 1, 1)
    pieces = jnp.concatenate([terms, second], axis=1).reshape(tcol, zh * own, rows + thin)
    pieces = exchange(pieces, "tcol")
    terms = pieces[:, :, :rows].sum(0)
    mine = lax.dynamic_slice(pieces, (2 * lax.axis_index("trow"), 0, rows), (2, zh * own, thin))
    pieces = jnp.concatenate([terms, mine[0], mine[1]], axis=1).reshape(zh, own, rows + 2 * thin)
    pieces = exchange(pieces, "zh")
    third = pieces[:, :, :rows].sum(0)
    second = pieces[:, :, rows:].reshape(zh, own, 2, thin).transpose(1, 2, 0, 3).reshape(own, rows)

    def norm(v):
        return jnp.sqrt(jnp.sum(v * v, axis=1))

    def inverse(x):
        return jnp.where(x > 0, 1.0 / jnp.where(x > 0, x, 1.0), 0.0)

    f0 = norm(first)
    e0 = first * inverse(f0)[:, None]
    s0 = jnp.sum(e0 * second, axis=1)
    rest = second - s0[:, None] * e0
    s1 = norm(rest)
    e1 = rest * inverse(s1)[:, None]
    t0 = jnp.sum(e0 * third, axis=1)
    t1 = jnp.sum(e1 * (third - t0[:, None] * e0), axis=1)
    f0, s0, s1, t0, t1 = jnp.moveaxis(spread(jnp.stack([f0, s0, s1, t0, t1]), "trow", trow), 1, 0)
    norm_first = jnp.sum(f0 * f0, 0)
    alpha = norm_first / jnp.sum(f0 * s0, 0)
    r0, r1 = (f0 - alpha * s0, -alpha * s1)
    norm_next = jnp.sum(r0 * r0 + r1 * r1, 0)
    beta = norm_next / norm_first
    d0, d1 = (r0 + beta * f0, r1)
    i0, i1 = (s0 - alpha * t0 + beta * s0, s1 - alpha * t1 + beta * s1)
    alpha_next = norm_next / jnp.sum(d0 * i0 + d1 * i1, 0)
    alpha, beta, alpha_next = (alpha[:, None], beta[:, None], alpha_next[:, None])
    residual = first - alpha * second
    direction = residual + beta * first
    image = second - alpha * third + beta * second
    merged = guess + alpha * first + alpha_next * direction
    return (merged, residual - alpha_next * image)


def solution(mesh):
    mp, trow, tcol = (mesh.shape[a] for a in ("mp", "trow", "tcol"))
    zl = 4 if mp % 4 == 0 and mp > 4 else 2
    sizes = {"zh": mp // zl, "zl": zl, "trow": trow, "tcol": tcol}
    split = Mesh(mesh.devices.reshape(tuple(sizes.values())), tuple(sizes))
    in_specs = (P(MP, "trow", "tcol"), P(MP + ("tcol",), "trow"), P(MP + ("tcol",), "trow"))
    out_specs = (P(MP + ("tcol",), "trow"), P(MP + ("tcol",), "trow"))

    def body(gram, rhs, guess):
        return shards(sizes, gram, rhs, guess)

    return jax.shard_map(body, mesh=split, in_specs=in_specs, out_specs=out_specs, check_vma=False)
```

profile of v0, /device:TPU:32, one launch (start us, length us, event | category | flops | bytes accessed | tf_op | source)
XLA Modules:
  0.0 201.9 jit_solution(11589484859543571213)
XLA Ops:
  7.2 1.9 reshape_squeeze.3
  9.2 1.6 copy.47
  10.8 0.7 copy-done.1
  11.4 0.6 collective-permute-start
  12.1 1.9 collective-permute-start.1
  14.0 1.1 collective-permute-done.1
  15.2 30.3 %all_to_all.50 = f32[16,2,2,512]{3,2,1,0:T(2,128)S(1)} all-to-all(f32[16,2,2,512]{3,2,1,0:T(2,128)S(1)} %broadcast_in_dim.21), channel_id=1, replica_groups=mesh['zh'=4,'zl'=4,'trow'=4,'tcol'=8] {'zh','zl'}, dimensions={0} | all-to-all | bytes 262144 | tf_op jit(solution)/shard_map/all_to_all | solution.py:22
  45.7 21.8 %all_to_all.51 = f32[4,64,512]{2,1,0:T(8,128)S(1)} all-to-all(f32[4,64,512]{2,1,0:T(8,128)S(1)} %broadcast_in_dim.23), channel_id=1, replica_groups=mesh['zh'=4,'zl'=4,'trow'=4,'tcol'=8] {'trow'}, dimensions={0} | all-to-all | bytes 1048576 | tf_op jit(solution)/shard_map/all_to_all | solution.py:22
  67.5 1.9 fusion
  69.5 18.5 %all_to_all.52 = f32[8,32,1024]{2,1,0:T(8,128)S(1)} all-to-all(f32[8,32,1024]{2,1,0:T(8,128)S(1)} %fusion), channel_id=1, replica_groups=mesh['zh'=4,'zl'=4,'trow'=4,'tcol'=8] {'tcol'}, dimensions={0} | all-to-all | bytes 2097152 | tf_op jit(solution)/shard_map/all_to_all | solution.py:22
  88.1 19.7 %all_to_all.53 = f32[16,2,1024]{2,1,0:T(2,128)S(1)} all-to-all(f32[16,2,1024]{2,1,0:T(2,128)S(1)} %reshape.100), channel_id=1, replica_groups=mesh['zh'=4,'zl'=4,'trow'=4,'tcol'=8] {'zh','zl'}, dimensions={0} | all-to-all | bytes 262144 | tf_op jit(solution)/shard_map/all_to_all | solution.py:22
  108.0 16.2 %all_to_all.54 = f32[4,2,1024]{2,1,0:T(2,128)S(1)} all-to-all(f32[4,2,1024]{2,1,0:T(2,128)S(1)} %broadcast_in_dim.24), channel_id=1, replica_groups=mesh['zh'=4,'zl'=4,'trow'=4,'tcol'=8] {'zh'}, dimensions={0} | all-to-all | bytes 65536 | tf_op jit(solution)/shard_map/all_to_all | solution.py:22
  124.2 0.7 broadcast_in_dim.26
  124.9 3.4 %all-to-all-start.5 = ((f32[8,8,1024]{2,1,0:T(8,128)}), f32[8,8,1024]{2,1,0:T(8,128)S(1)}, u32[]{:S(2)}, u32[]{:S(2)}) async-start(f32[8,8,1024]{2,1,0:T(8,128)} %broadcast_in_dim.26), calls=%async_computation.5 | async-start | bytes 524288 | tf_op jit(solution)/shard_map/all_to_all | solution.py:22
  128.4 16.4 %all_gather.3 = f32[1024,128]{1,0:T(8,128)S(1)} all-gather(f32[256,128]{1,0:T(8,128)} %reduce-scatter.2.cloned.1.call-done), channel_id=1, replica_groups=mesh['zh'=4,'zl'=4,'trow'=4,'tcol'=8] {'zl'}, dimensions={0}, use_global_device_ids=true | all-gather | bytes 655360 | tf_op jit(solution)/shard_map/all_gather | solution.py:62
  145.3 8.4 %all_to_all.55 = f32[4,64,128]{2,1,0:T(8,128)S(1)} all-to-all(f32[4,64,128]{2,1,0:T(8,128)S(1)} %broadcast_in_dim.27), channel_id=1, replica_groups=mesh['zh'=4,'zl'=4,'trow'=4,'tcol'=8] {'trow'}, dimensions={0} | all-to-all | bytes 262144 | tf_op jit(solution)/shard_map/all_to_all | solution.py:22
  153.6 0.7 fusion.21
  154.3 0.7 maximum_bitcast_fusion
  155.0 4.7 %all-to-all-start.7 = ((f32[8,8,1152]{2,1,0:T(8,128)}), f32[8,8,1152]{2,1,0:T(8,128)S(1)}, u32[]{:S(2)}, u32[]{:S(2)}) async-start(f32[8,8,1152]{2,1,0:T(8,128)} %maximum_bitcast_fusion), calls=%async_computation.8 | async-start | bytes 589824 | tf_op jit(solution)/shard_map/all_to_all | solution.py:22
  159.8 7.9 %all-to-all-done.7 = f32[8,8,1152]{2,1,0:T(8,128)S(1)} async-done(((f32[8,8,1152]{2,1,0:T(8,128)}), f32[8,8,1152]{2,1,0:T(8,128)S(1)}, u32[]{:S(2)}, u32[]{:S(2)}) %all-to-all-start.7) | async-done | bytes 294944 | tf_op jit(solution)/shard_map/all_to_all | solution.py:22
  168.4 3.3 %all-to-all-start.8 = ((f32[4,2,1280]{2,1,0:T(2,128)}), f32[4,2,1280]{2,1,0:T(2,128)S(1)}, u32[]{:S(2)}, u32[]{:S(2)}) async-start(f32[4,2,1280]{2,1,0:T(2,128)} %pad_maximum_fusion), calls=%async_computation.9 | async-start | bytes 81920 | tf_op jit(solution)/shard_map/all_to_all | solution.py:22
  171.8 12.7 %all-to-all-done.8 = f32[4,2,1280]{2,1,0:T(2,128)S(1)} async-done(((f32[4,2,1280]{2,1,0:T(2,128)}), f32[4,2,1280]{2,1,0:T(2,128)S(1)}, u32[]{:S(2)}, u32[]{:S(2)}) %all-to-all-start.8) | async-done | bytes 40992 | tf_op jit(solution)/shard_map/all_to_all | solution.py:22
  185.6 7.6 %all_to_all.56 = f32[4,5,2]{1,2,0:T(2,128)S(1)} all-to-all(f32[4,5,2]{1,2,0:T(2,128)S(1)} %broadcast_in_dim.28), channel_id=1, replica_groups=mesh['zh'=4,'zl'=4,'trow'=4,'tcol'=8] {'trow'}, dimensions={0} | all-to-all | bytes 320 | tf_op jit(solution)/shard_map/all_to_all | solution.py:22
  194.4 0.7 multiply_subtract_fusion
  (59 shorter events, 4.2 us)
Async XLA Ops:
  7.2 121.2 %reduce-scatter.2.cloned.1.call-start = ((), (), s32[]{:S(2)}) async-start(), calls=%async_computation.11 | async-start | bytes 2228224 | tf_op jit(solution)/shard_map/reduce_scatter | solution.py:61
  10.7 0.7 copy-start.1
  10.7 56.8 %copy-start = (f32[1,1024,512]{2,1,0:T(8,128)S(1)}, f32[1,1024,512]{2,1,0:T(8,128)}, u32[]{:S(2)}) copy-start(f32[1,1024,512]{2,1,0:T(8,128)} %param.3) | copy-start | bytes 6291460
  11.4 2.6 %collective-permute-start = (f32[2,512]{1,0:T(2,128)S(1)}, f32[2,512]{1,0:T(2,128)S(1)}, u32[]{:S(2)}, u32[]{:S(2)}) collective-permute-start(f32[2,512]{1,0:T(2,128)S(1)} %get-tuple-element.16), channel_id=1, source_target_pairs={{0,0},{1,1},{2,8},{3,9},{4,16},{5,17},{6,24},{7,25},{8,2},{9,3},{1... | collective-permute-start | bytes 12296 | tf_op jit(solution)/shard_map/ppermute | solution.py:44
  12.1 3.1 %collective-permute-start.1 = (f32[2,512]{1,0:T(2,128)S(1)}, f32[2,512]{1,0:T(2,128)S(1)}, u32[]{:S(2)}, u32[]{:S(2)}) collective-permute-start(f32[2,512]{1,0:T(2,128)S(1)} %get-tuple-element.17), channel_id=1, source_target_pairs={{0,1},{1,0},{2,9},{3,8},{4,17},{5,16},{6,25},{7,24},{8,3},{9,2},{1... | collective-permute-start | bytes 12296 | tf_op jit(solution)/shard_map/ppermute | solution.py:44
  69.5 38.4 %copy-start.2 = (f32[2,1024]{1,0:T(2,128)S(1)}, f32[2,1024]{1,0:T(2,128)}, u32[]{:S(2)}) copy-start(f32[2,1024]{1,0:T(2,128)} %param.4) | copy-start | bytes 24580
  124.9 19.9 %all-to-all-start.5 = ((f32[8,8,1024]{2,1,0:T(8,128)}), f32[8,8,1024]{2,1,0:T(8,128)S(1)}, u32[]{:S(2)}, u32[]{:S(2)}) async-start(f32[8,8,1024]{2,1,0:T(8,128)} %broadcast_in_dim.26), calls=%async_computation.5 | async-start | bytes 524288 | tf_op jit(solution)/shard_map/all_to_all | solution.py:22
  155.0 12.6 %all-to-all-start.7 = ((f32[8,8,1152]{2,1,0:T(8,128)}), f32[8,8,1152]{2,1,0:T(8,128)S(1)}, u32[]{:S(2)}, u32[]{:S(2)}) async-start(f32[8,8,1152]{2,1,0:T(8,128)} %maximum_bitcast_fusion), calls=%async_computation.8 | async-start | bytes 589824 | tf_op jit(solution)/shard_map/all_to_all | solution.py:22
  168.4 16.1 %all-to-all-start.8 = ((f32[4,2,1280]{2,1,0:T(2,128)}), f32[4,2,1280]{2,1,0:T(2,128)S(1)}, u32[]{:S(2)}, u32[]{:S(2)}) async-start(f32[4,2,1280]{2,1,0:T(2,128)} %pad_maximum_fusion), calls=%async_computation.9 | async-start | bytes 81920 | tf_op jit(solution)/shard_map/all_to_all | solution.py:22
Sparse Core Ops, SparseCore 0:
  10.9 80.2 reduce-scatter.1
where the time goes:
time: 203 us; the launch traced here: 202 us
  blocking collectives  139 us (68%)
  waiting for transfers between devices  21.7 us (11%)
  between operations  14.3 us (7%)
  starting transfers between devices  14 us (7%)
  local copies, waits for them, and re-layouts  6.45 us (3%)
  other arithmetic  3.55 us (2%)
  matrix products  3.02 us (1%)
    all_to_all x7, blocking collectives, exchange(): return lax.all_to_all(pieces, axes, 0, 0, tiled=True)  122 us
    all_to_all x3, waiting for transfers between devices, exchange(): return lax.all_to_all(pieces, axes, 0, 0, tiled=True)  20.6 us
    all_gather x1, blocking collectives, shards(): total = lax.all_gather(part, 'zl', axis=0, tiled=True)  16.4 us
    all_to_all x3, starting transfers between devices, exchange(): return lax.all_to_all(pieces, axes, 0, 0, tiled=True)  11.4 us
  transfers between devices with their start and end apart: 6, of which 3 were waited for; matrix products, arithmetic and copies ran while one was open for 2% of the time, Pallas kernels for 0%

commit v1 on v0

--- a/solution.py
+++ b/solution.py
@@ -59,7 +59,8 @@
         .reshape(mp * (rows // zl), thin)
     )
     part = lax.psum_scatter(cut, MP, scatter_dimension=0, tiled=True)
-    total = lax.all_gather(part, "zl", axis=0, tiled=True)
+    outgoing = jnp.stack([part] * lax.axis_size("zl"))
+    total = jnp.concatenate(lax.all_to_all(outgoing, "zl", 0, 0), axis=0)
     flipped = transposed(guess, sizes)
     over_mp = spread(flipped, MP, mp)
     over_mp = over_mp.transpose(1, 0, 2, 3).reshape(2 * mp * own, cols)

time: 203 us -> 210 us (1.034)
  the two profiles are of different devices: /device:TPU:32 before, /device:TPU:2 now
where the time goes in v1:
time: 210 us; the launch traced here: 209 us
  blocking collectives  145 us (69%)
  waiting for transfers between devices  23.9 us (11%)
  between operations  14.3 us (7%)
  starting transfers between devices  12.6 us (6%)
  local copies, waits for them, and re-layouts  6.66 us (3%)
  other arithmetic  3.55 us (2%)
  matrix products  3.02 us (1%)
    all_to_all x8, blocking collectives, exchange(): return lax.all_to_all(pieces, axes, 0, 0, tiled=True)  127 us
    all_to_all x2, waiting for transfers between devices, exchange(): return lax.all_to_all(pieces, axes, 0, 0, tiled=True)  20.5 us
    all_to_all x1, blocking collectives, shards(): total = jnp.concatenate(lax.all_to_all(outgoing, 'zl', 0, 0), axis=0)  18.1 us
    all_to_all x2, starting transfers between devices, exchange(): return lax.all_to_all(pieces, axes, 0, 0, tiled=True)  6.69 us
    ppermute x2, starting transfers between devices, transposed(): got.append(lax.ppermute(sent, PLANE, pairs))  5.89 us
  transfers between devices with their start and end apart: 5, of which 4 were waited for; matrix products, arithmetic and copies ran while one was open for 1% of the time, Pallas kernels for 0%

profile of v1, /device:TPU:2, one launch (start us, length us, event | category | flops | bytes accessed | tf_op | source)
XLA Modules:
  0.0 208.9 jit_solution(7347073448690327831)
XLA Ops:
  7.2 1.9 reshape_squeeze.3
  9.2 1.6 copy.47
  10.8 0.7 copy-done.1
  11.4 3.4 %collective-permute-start = (f32[2,512]{1,0:T(2,128)S(1)}, f32[2,512]{1,0:T(2,128)S(1)}, u32[]{:S(2)}, u32[]{:S(2)}) collective-permute-start(f32[2,512]{1,0:T(2,128)S(1)} %get-tuple-element.16), channel_id=1, source_target_pairs={{0,0},{1,1},{2,8},{3,9},{4,16},{5,17},{6,24},{7,25},{8,2},{9,3},{1... | collective-permute-start | bytes 12296 | tf_op jit(solution)/shard_map/ppermute | solution.py:44
  14.9 2.4 %collective-permute-start.1 = (f32[2,512]{1,0:T(2,128)S(1)}, f32[2,512]{1,0:T(2,128)S(1)}, u32[]{:S(2)}, u32[]{:S(2)}) collective-permute-start(f32[2,512]{1,0:T(2,128)S(1)} %get-tuple-element.17), channel_id=1, source_target_pairs={{0,1},{1,0},{2,9},{3,8},{4,17},{5,16},{6,25},{7,24},{8,3},{9,2},{1... | collective-permute-start | bytes 12296 | tf_op jit(solution)/shard_map/ppermute | solution.py:44
  17.8 2.9 %collective-permute-done.1 = f32[2,512]{1,0:T(2,128)S(1)} collective-permute-done((f32[2,512]{1,0:T(2,128)S(1)}, f32[2,512]{1,0:T(2,128)S(1)}, u32[]{:S(2)}, u32[]{:S(2)}) %collective-permute-start.1) | collective-permute-done | bytes 4128 | tf_op jit(solution)/shard_map/ppermute | solution.py:44
  20.8 31.4 %all_to_all.55 = f32[16,2,2,512]{3,2,1,0:T(2,128)S(1)} all-to-all(f32[16,2,2,512]{3,2,1,0:T(2,128)S(1)} %broadcast_in_dim.21), channel_id=1, replica_groups=mesh['zh'=4,'zl'=4,'trow'=4,'tcol'=8] {'zh','zl'}, dimensions={0} | all-to-all | bytes 262144 | tf_op jit(solution)/shard_map/all_to_all | solution.py:22
  52.3 14.4 %all_to_all.56 = f32[4,64,512]{2,1,0:T(8,128)S(1)} all-to-all(f32[4,64,512]{2,1,0:T(8,128)S(1)} %broadcast_in_dim.23), channel_id=1, replica_groups=mesh['zh'=4,'zl'=4,'trow'=4,'tcol'=8] {'trow'}, dimensions={0} | all-to-all | bytes 1048576 | tf_op jit(solution)/shard_map/all_to_all | solution.py:22
  66.7 1.9 fusion
  68.7 18.5 %all_to_all.57 = f32[8,32,1024]{2,1,0:T(8,128)S(1)} all-to-all(f32[8,32,1024]{2,1,0:T(8,128)S(1)} %fusion), channel_id=1, replica_groups=mesh['zh'=4,'zl'=4,'trow'=4,'tcol'=8] {'tcol'}, dimensions={0} | all-to-all | bytes 2097152 | tf_op jit(solution)/shard_map/all_to_all | solution.py:22
  87.4 20.0 %all_to_all.58 = f32[16,2,1024]{2,1,0:T(2,128)S(1)} all-to-all(f32[16,2,1024]{2,1,0:T(2,128)S(1)} %reshape.105), channel_id=1, replica_groups=mesh['zh'=4,'zl'=4,'trow'=4,'tcol'=8] {'zh','zl'}, dimensions={0} | all-to-all | bytes 262144 | tf_op jit(solution)/shard_map/all_to_all | solution.py:22
  107.5 16.6 %all_to_all.59 = f32[4,2,1024]{2,1,0:T(2,128)S(1)} all-to-all(f32[4,2,1024]{2,1,0:T(2,128)S(1)} %broadcast_in_dim.24), channel_id=1, replica_groups=mesh['zh'=4,'zl'=4,'trow'=4,'tcol'=8] {'zh'}, dimensions={0} | all-to-all | bytes 65536 | tf_op jit(solution)/shard_map/all_to_all | solution.py:22
  124.2 9.9 %all_to_all.60 = f32[8,8,1024]{2,1,0:T(8,128)S(1)} all-to-all(f32[8,8,1024]{2,1,0:T(8,128)S(1)} %broadcast_in_dim.26), channel_id=1, replica_groups=mesh['zh'=4,'zl'=4,'trow'=4,'tcol'=8] {'tcol'}, dimensions={0} | all-to-all | bytes 524288 | tf_op jit(solution)/shard_map/all_to_all | solution.py:22
  134.1 0.9 stack.33
  135.1 18.1 %all_to_all.61 = f32[4,256,128]{2,1,0:T(8,128)S(1)} all-to-all(f32[4,256,128]{2,1,0:T(8,128)S(1)} %stack.33), channel_id=1, replica_groups=mesh['zh'=4,'zl'=4,'trow'=4,'tcol'=8] {'zl'}, dimensions={0} | all-to-all | bytes 1048576 | tf_op jit(solution)/shard_map/all_to_all | solution.py:63
  153.6 8.4 %all_to_all.62 = f32[4,64,128]{2,1,0:T(8,128)S(1)} all-to-all(f32[4,64,128]{2,1,0:T(8,128)S(1)} %broadcast_in_dim.27), channel_id=1, replica_groups=mesh['zh'=4,'zl'=4,'trow'=4,'tcol'=8] {'trow'}, dimensions={0} | all-to-all | bytes 262144 | tf_op jit(solution)/shard_map/all_to_all | solution.py:22
  162.0 0.7 fusion.21
  162.7 0.7 maximum_bitcast_fusion
  163.4 3.4 %all-to-all-start.8 = ((f32[8,8,1152]{2,1,0:T(8,128)}), f32[8,8,1152]{2,1,0:T(8,128)S(1)}, u32[]{:S(2)}, u32[]{:S(2)}) async-start(f32[8,8,1152]{2,1,0:T(8,128)} %maximum_bitcast_fusion), calls=%async_computation.9 | async-start | bytes 589824 | tf_op jit(solution)/shard_map/all_to_all | solution.py:22
  166.9 7.8 %all-to-all-done.8 = f32[8,8,1152]{2,1,0:T(8,128)S(1)} async-done(((f32[8,8,1152]{2,1,0:T(8,128)}), f32[8,8,1152]{2,1,0:T(8,128)S(1)}, u32[]{:S(2)}, u32[]{:S(2)}) %all-to-all-start.8) | async-done | bytes 294944 | tf_op jit(solution)/shard_map/all_to_all | solution.py:22
  175.4 3.3 %all-to-all-start.9 = ((f32[4,2,1280]{2,1,0:T(2,128)}), f32[4,2,1280]{2,1,0:T(2,128)S(1)}, u32[]{:S(2)}, u32[]{:S(2)}) async-start(f32[4,2,1280]{2,1,0:T(2,128)} %pad_maximum_fusion), calls=%async_computation.10 | async-start | bytes 81920 | tf_op jit(solution)/shard_map/all_to_all | solution.py:22
  178.7 12.7 %all-to-all-done.9 = f32[4,2,1280]{2,1,0:T(2,128)S(1)} async-done(((f32[4,2,1280]{2,1,0:T(2,128)}), f32[4,2,1280]{2,1,0:T(2,128)S(1)}, u32[]{:S(2)}, u32[]{:S(2)}) %all-to-all-start.9) | async-done | bytes 40992 | tf_op jit(solution)/shard_map/all_to_all | solution.py:22
  192.6 7.6 %all_to_all.63 = f32[4,5,2]{1,2,0:T(2,128)S(1)} all-to-all(f32[4,5,2]{1,2,0:T(2,128)S(1)} %broadcast_in_dim.28), channel_id=1, replica_groups=mesh['zh'=4,'zl'=4,'trow'=4,'tcol'=8] {'trow'}, dimensions={0} | all-to-all | bytes 320 | tf_op jit(solution)/shard_map/all_to_all | solution.py:22
  201.4 0.7 multiply_subtract_fusion
  (59 shorter events, 4.7 us)
Async XLA Ops:
  7.2 127.0 %reduce-scatter.2.cloned.1.call-start = ((), (), s32[]{:S(2)}) async-start(), calls=%async_computation.12 | async-start | bytes 2228224 | tf_op jit(solution)/shard_map/reduce_scatter | solution.py:61
  10.7 0.7 copy-start.1
  10.7 56.0 %copy-start = (f32[1,1024,512]{2,1,0:T(8,128)S(1)}, f32[1,1024,512]{2,1,0:T(8,128)}, u32[]{:S(2)}) copy-start(f32[1,1024,512]{2,1,0:T(8,128)} %param.3) | copy-start | bytes 6291460
  11.4 6.4 %collective-permute-start = (f32[2,512]{1,0:T(2,128)S(1)}, f32[2,512]{1,0:T(2,128)S(1)}, u32[]{:S(2)}, u32[]{:S(2)}) collective-permute-start(f32[2,512]{1,0:T(2,128)S(1)} %get-tuple-element.16), channel_id=1, source_target_pairs={{0,0},{1,1},{2,8},{3,9},{4,16},{5,17},{6,24},{7,25},{8,2},{9,3},{1... | collective-permute-start | bytes 12296 | tf_op jit(solution)/shard_map/ppermute | solution.py:44
  14.9 5.8 %collective-permute-start.1 = (f32[2,512]{1,0:T(2,128)S(1)}, f32[2,512]{1,0:T(2,128)S(1)}, u32[]{:S(2)}, u32[]{:S(2)}) collective-permute-start(f32[2,512]{1,0:T(2,128)S(1)} %get-tuple-element.17), channel_id=1, source_target_pairs={{0,1},{1,0},{2,9},{3,8},{4,17},{5,16},{6,25},{7,24},{8,3},{9,2},{1... | collective-permute-start | bytes 12296 | tf_op jit(solution)/shard_map/ppermute | solution.py:44
  68.7 38.7 %copy-start.2 = (f32[2,1024]{1,0:T(2,128)S(1)}, f32[2,1024]{1,0:T(2,128)}, u32[]{:S(2)}) copy-start(f32[2,1024]{1,0:T(2,128)} %param.4) | copy-start | bytes 24580
  163.4 11.2 %all-to-all-start.8 = ((f32[8,8,1152]{2,1,0:T(8,128)}), f32[8,8,1152]{2,1,0:T(8,128)S(1)}, u32[]{:S(2)}, u32[]{:S(2)}) async-start(f32[8,8,1152]{2,1,0:T(8,128)} %maximum_bitcast_fusion), calls=%async_computation.9 | async-start | bytes 589824 | tf_op jit(solution)/shard_map/all_to_all | solution.py:22
  175.4 16.1 %all-to-all-start.9 = ((f32[4,2,1280]{2,1,0:T(2,128)}), f32[4,2,1280]{2,1,0:T(2,128)S(1)}, u32[]{:S(2)}, u32[]{:S(2)}) async-start(f32[4,2,1280]{2,1,0:T(2,128)} %pad_maximum_fusion), calls=%async_computation.10 | async-start | bytes 81920 | tf_op jit(solution)/shard_map/all_to_all | solution.py:22
Sparse Core Ops, SparseCore 0:
  10.9 81.6 reduce-scatter.1
